TPU v7x, 32 devices: a whole 2x2x4 slice. The times are simulated.
32 devices in a mesh: clus: 8 (over z, y), rep: 4 (over x, core).
Axes of the slice: x: 2, y: 2, z: 4, core: 2. Of those that a mesh axis runs over, the one named last changes fastest.
Arguments:
- embeddings: bfloat16 [2048, 1024], P(('clus', 'rep')), may hold values from -700 to 700
- inv_temp: bfloat16 [2048], P(('clus', 'rep')), may hold values from 16 to 256
- routes: int32 [2048, 3], P(('clus', 'rep')), may hold values from 0 to 6, all different within a row; in each aligned block of 64 rows (0 to 63, 64 to 127, ...) at most 34 rows name the same one
Outputs:
- dup_score: float32 [2048], P(('clus', 'rep'))
Inputs may be any that keep to these rules, and one draw needn't show every extreme that they name: `routes`: the values of one row are distinct. Within the rows of one device no value stands in more than 34 rows, and in some device one value stands in exactly 34 rows.
All inputs are finite; a program needn't handle non-finite values.
Results may differ from a plain program's by a relative error of at most 0.00051.
Values may be sent and summed in bfloat16 or wider, within the bound.
A program may use at most 64 MiB of HBM per device.

v0:
```python
import jax
import jax.numpy as jnp
from jax import lax
from jax.sharding import PartitionSpec as P

EPS = 1e-06


def unit_rows(values):
    widened = values.astype(jnp.float32)
    scale = lax.rsqrt(jnp.sum(widened * widened, axis=1, keepdims=True) + EPS)
    return (widened * scale).astype(jnp.bfloat16)


def block_stats(queries, inverse, key_rows, self_mask):
    scores = jnp.einsum("qd,kd->qk", queries, key_rows, preferred_element_type=jnp.float32)
    scores = scores * inverse.astype(jnp.float32)[:, None]
    if self_mask is not None:
        scores = jnp.where(self_mask, -jnp.inf, scores)
    top_score = jnp.max(scores, axis=1)
    exp_mass = jnp.sum(jnp.exp(scores - top_score[:, None]), axis=1)
    return (top_score, exp_mass)


def per_device(embeddings, inv_temp, routes):
    row_count, feature_width = embeddings.shape
    neighbours = routes.shape[1]
    owners = lax.axis_size("clus")
    replicas = lax.axis_size("rep")
    owner_self = lax.axis_index("clus")
    replica_self = lax.axis_index("rep")
    capacity = min(
        row_count,
        max(
            2,
            (row_count * neighbours + owners - 2) // (owners - 1)
            + row_count * neighbours // (4 * (owners - 1)),
        ),
    )
    normalized = unit_rows(embeddings)
    local_ids = jnp.arange(row_count, dtype=jnp.int32)
    cluster_ids = jnp.arange(row_count * replicas, dtype=jnp.int32)
    cluster_keys = lax.all_gather(normalized, "rep", axis=0, tiled=True)
    own_mask = cluster_ids[None, :] == (replica_self * row_count + local_ids)[:, None]
    own_top, own_mass = block_stats(normalized, inv_temp, cluster_keys, own_mask)
    targets = (owner_self + 1 + routes) % owners
    owner_ids = jnp.arange(owners, dtype=jnp.int32)
    target_hits = jnp.sum(
        (targets[:, :, None] == owner_ids[None, None, :]).astype(jnp.int32), axis=1
    )
    earlier_hits = jnp.cumsum(target_hits, axis=0) - target_hits
    slot_index = jnp.take_along_axis(earlier_hits, targets, axis=1)
    row_ids = jnp.broadcast_to(local_ids[:, None], targets.shape)
    source_table = jnp.zeros((owners, capacity), jnp.int32).at[targets, slot_index].set(row_ids)
    filled = (
        jnp.zeros((owners, capacity), jnp.bfloat16).at[targets, slot_index].set(jnp.bfloat16(1.0))
    )
    visitor_rows = normalized[source_table] * filled[:, :, None]
    visitor_inverse = inv_temp[source_table] * filled
    arrived = lax.all_to_all(visitor_rows, "clus", split_axis=0, concat_axis=0, tiled=True)
    arrived_inverse = lax.all_to_all(
        visitor_inverse, "clus", split_axis=0, concat_axis=0, tiled=True
    )
    senders = arrived.shape[0]
    item_count = arrived.shape[1]
    top_score, exp_mass = block_stats(
        arrived.reshape(senders * item_count, feature_width),
        arrived_inverse.reshape(senders * item_count),
        cluster_keys,
        None,
    )
    top_score = top_score.reshape(senders, item_count)
    exp_mass = exp_mass.reshape(senders, item_count)
    near_top = lax.all_to_all(top_score, "clus", split_axis=0, concat_axis=0, tiled=True)
    near_mass = lax.all_to_all(exp_mass, "clus", split_axis=0, concat_axis=0, tiled=True)
    picked_top = near_top[targets, slot_index]
    picked_mass = near_mass[targets, slot_index]
    highest = jnp.maximum(own_top, jnp.max(picked_top, axis=1))
    sum_total = own_mass * jnp.exp(own_top - highest) + jnp.sum(
        picked_mass * jnp.exp(picked_top - highest[:, None]), axis=1
    )
    return (highest + jnp.log(sum_total)) / inv_temp.astype(jnp.float32)


def solution(mesh):
    in_specs = (P(("clus", "rep"), None), P(("clus", "rep")), P(("clus", "rep"), None))
    out_specs = P(("clus", "rep"))
    return jax.shard_map(
        per_device, mesh=mesh, in_specs=in_specs, out_specs=out_specs, check_vma=False
    )
```

profile of v0, /device:TPU:0, one launch (start us, length us, event | category | flops | bytes accessed | tf_op | source)
XLA Modules:
  0.0 82.4 jit_solution(11016803126296305307)
XLA Ops:
  0.0 0.7 copy-done.2
  0.7 0.1 copy.8
  0.8 0.1 copy.9
  0.9 0.1 copy.10
  1.0 0.1 reduce_window_sum.11
  1.1 0.1 reshape.83
  1.2 1.6 %gather_fusion.4 = s32[192]{0:T(256)S(1)} fusion(s32[64,8]{1,0:T(8,128)S(1)} %sub.30, s32[192]{0:T(256)S(1)} %reshape.83), kind=kCustom, calls=%fused_computation.4 | custom fusion | bytes 3072 | tf_op jit(solution)/shard_map/jit(take_along_axis)/gather | solution.py:52
  2.9 0.1 reshape.86
  3.0 0.1 reshape.89
  3.2 0.1 reshape.91
  3.3 0.0 copy-start
  3.3 9.3 %scatter_fusion = s32[8,34]{1,0:T(8,128)S(1)} fusion(s32[8,34]{1,0:T(8,128)S(1)} %broadcast.39, s32[192]{0:T(256)S(1)} %reshape.89, s32[192]{0:T(256)S(1)} %reshape.91), kind=kCustom, calls=%fused_computation.5 | custom fusion | bytes 3840 | tf_op jit(solution)/shard_map/scatter | solution.py:54
  12.6 0.1 reshape.57
  12.7 2.4 %gather_fusion.1 = bf16[272]{0:T(512)(128)(2,1)S(1)} fusion(bf16[64]{0:T(256)(128)(2,1)S(1)} %copy-done, s32[1024]{0:T(1024)S(1)} %pad_clamp_fusion), kind=kCustom, calls=%fused_computation.1 | custom fusion | bytes 2176 | tf_op jit(solution)/shard_map/gather | solution.py:59
  15.1 0.1 reshape.64
  15.2 0.0 copy-start.1
  15.2 9.5 %scatter_fusion.1 = bf16[8,34]{1,0:T(8,128)(2,1)S(1)} fusion(bf16[8,34]{1,0:T(8,128)(2,1)S(1)} %broadcast_in_dim.23, s32[192]{0:T(256)S(1)} %reshape.89, bf16[192]{0:T(256)(128)(2,1)S(1)} %broadcast.115), kind=kCustom, calls=%fused_computation.6 | custom fusion | bytes 2688 | tf_op jit(solution)/shard_map/scatter | solution.py:56
  24.7 0.6 copy.12
  25.3 7.3 %all-to-all-start.1 = ((bf16[8,1,34]{2,1,0:T(2,128)(2,1)}), bf16[8,1,34]{2,1,0:T(2,128)(2,1)S(1)}, u32[]{:S(2)}, u32[]{:S(2)}) async-start(bf16[8,1,34]{2,1,0:T(2,128)(2,1)} %copy.12), calls=%async_computation.1 | async-start | bytes 8192 | tf_op jit(solution)/shard_map/all_to_all | solution.py:61
  32.6 0.1 fusion.1
  32.7 0.1 fusion.2
  32.8 2.1 %gather_fusion = bf16[272,1024]{1,0:T(8,128)(2,1)S(1)} fusion(bf16[64,1024]{1,0:T(8,128)(2,1)S(1)} %fusion.2, s32[1024]{0:T(1024)S(1)} %pad_clamp_fusion), kind=kCustom, calls=%fused_computation | custom fusion | bytes 1115200 | tf_op jit(solution)/shard_map/gather | solution.py:58
  34.9 0.2 reshape.56
  35.1 0.9 %broadcast_multiply_fusion = bf16[8,34,1024]{2,1,0:T(8,128)(2,1)} fusion(bf16[8,34,1024]{2,1,0:T(8,128)(2,1)S(1)} %reshape.56, bf16[8,34]{1,0:T(8,128)(2,1)S(1)} %scatter_fusion.1), kind=kLoop, calls=%fused_computation.12 | loop fusion | flops 278528 | bytes 1114656 | tf_op jit(solution)/shard_map/mul | solution.py:58
  36.0 3.0 %all-to-all-done.1 = bf16[8,1,34]{2,1,0:T(2,128)(2,1)S(1)} async-done(((bf16[8,1,34]{2,1,0:T(2,128)(2,1)}), bf16[8,1,34]{2,1,0:T(2,128)(2,1)S(1)}, u32[]{:S(2)}, u32[]{:S(2)}) %all-to-all-start.1) | async-done | bytes 576 | tf_op jit(solution)/shard_map/all_to_all | solution.py:61
  39.1 3.5 %all-to-all-start = ((bf16[8,34,1024]{2,1,0:T(8,128)(2,1)}), bf16[8,34,1024]{2,1,0:T(8,128)(2,1)S(1)}, u32[]{:S(2)}, u32[]{:S(2)}) async-start(bf16[8,34,1024]{2,1,0:T(8,128)(2,1)} %broadcast_multiply_fusion), calls=%async_computation | async-start | bytes 1310720 | tf_op jit(solution)/shard_map/all_to_all | solution.py:60
  42.6 7.2 %all_gather.3 = bf16[256,1024]{1,0:T(8,128)(2,1)S(1)} all-gather(bf16[64,1024]{1,0:T(8,128)(2,1)S(1)} %fusion.2), channel_id=1, replica_groups=mesh['clus'=8,'rep'=4] {'rep'}, dimensions={0}, use_global_device_ids=true | all-gather | bytes 655360 | tf_op jit(solution)/shard_map/all_gather | solution.py:43
  49.8 0.1 reshape.54
  49.9 8.9 %all-to-all-done = bf16[8,34,1024]{2,1,0:T(8,128)(2,1)S(1)} async-done(((bf16[8,34,1024]{2,1,0:T(8,128)(2,1)}), bf16[8,34,1024]{2,1,0:T(8,128)(2,1)S(1)}, u32[]{:S(2)}, u32[]{:S(2)}) %all-to-all-start) | async-done | bytes 557088 | tf_op jit(solution)/shard_map/all_to_all | solution.py:60
  58.8 0.2 reshape.53
  59.0 0.5 fusion.10
  59.4 0.2 exponential_reduce_fusion
  59.7 0.7 all_to_all.31
  60.3 3.6 %all-to-all-start.3 = ((f32[8,1,34]{2,1,0:T(1,128)}), f32[8,1,34]{2,1,0:T(1,128)S(1)}, u32[]{:S(2)}, u32[]{:S(2)}) async-start(f32[8,1,34]{2,1,0:T(1,128)} %all_to_all.31), calls=%async_computation.3 | async-start | bytes 8192 | tf_op jit(solution)/shard_map/all_to_all | solution.py:75
  64.0 0.4 fusion.9
  64.4 0.7 all_to_all.28
  65.0 5.4 %all-to-all-done.3 = f32[8,1,34]{2,1,0:T(1,128)S(1)} async-done(((f32[8,1,34]{2,1,0:T(1,128)}), f32[8,1,34]{2,1,0:T(1,128)S(1)}, u32[]{:S(2)}, u32[]{:S(2)}) %all-to-all-start.3) | async-done | bytes 1120 | tf_op jit(solution)/shard_map/all_to_all | solution.py:75
  70.4 3.3 %all-to-all-start.2 = ((f32[8,1,34]{2,1,0:T(1,128)}), f32[8,1,34]{2,1,0:T(1,128)S(1)}, u32[]{:S(2)}, u32[]{:S(2)}) async-start(f32[8,1,34]{2,1,0:T(1,128)} %all_to_all.28), calls=%async_computation.2 | async-start | bytes 8192 | tf_op jit(solution)/shard_map/all_to_all | solution.py:74
  73.8 0.2 exponential_reduce_fusion.1
  74.0 0.1 reshape.71
  74.1 1.2 %gather_fusion.3 = f32[192]{0:T(256)S(1)} fusion(f32[8,34]{1,0:T(8,128)S(1)} %bitcast.32, s32[192]{0:T(256)S(1)} %reshape.71), kind=kCustom, calls=%fused_computation.3 | custom fusion | bytes 3072 | tf_op jit(solution)/shard_map/gather | solution.py:77
  75.3 0.1 reshape.80
  75.5 4.7 %all-to-all-done.2 = f32[8,1,34]{2,1,0:T(1,128)S(1)} async-done(((f32[8,1,34]{2,1,0:T(1,128)}), f32[8,1,34]{2,1,0:T(1,128)S(1)}, u32[]{:S(2)}, u32[]{:S(2)}) %all-to-all-start.2) | async-done | bytes 1120 | tf_op jit(solution)/shard_map/all_to_all | solution.py:74
  80.2 1.2 %gather_fusion.2 = f32[192]{0:T(256)S(1)} fusion(f32[8,34]{1,0:T(8,128)S(1)} %bitcast.33, s32[192]{0:T(256)S(1)} %reshape.71), kind=kCustom, calls=%fused_computation.2 | custom fusion | bytes 3072 | tf_op jit(solution)/shard_map/gather | solution.py:76
  81.4 0.1 reshape.74
  81.5 0.1 reduce_max.29
  81.7 0.2 multiply_reduce_fusion
  81.8 0.5 add_divide_fusion
  (19 shorter events, 0.2 us)
Async XLA Ops:
  0.0 0.7 copy-start.2
  3.3 9.4 %copy-start = (bf16[64]{0:T(256)(128)(2,1)S(1)}, bf16[64]{0:T(256)(128)(2,1)}, u32[]{:S(2)}) copy-start(bf16[64]{0:T(256)(128)(2,1)} %param.4) | copy-start | bytes 388
  15.2 17.4 %copy-start.1 = (bf16[64,1024]{1,0:T(8,128)(2,1)S(1)}, bf16[64,1024]{1,0:T(8,128)(2,1)}, u32[]{:S(2)}) copy-start(bf16[64,1024]{1,0:T(8,128)(2,1)} %param.3) | copy-start | bytes 393220
  25.3 13.7 %all-to-all-start.1 = ((bf16[8,1,34]{2,1,0:T(2,128)(2,1)}), bf16[8,1,34]{2,1,0:T(2,128)(2,1)S(1)}, u32[]{:S(2)}, u32[]{:S(2)}) async-start(bf16[8,1,34]{2,1,0:T(2,128)(2,1)} %copy.12), calls=%async_computation.1 | async-start | bytes 8192 | tf_op jit(solution)/shard_map/all_to_all | solution.py:61
  39.1 19.7 %all-to-all-start = ((bf16[8,34,1024]{2,1,0:T(8,128)(2,1)}), bf16[8,34,1024]{2,1,0:T(8,128)(2,1)S(1)}, u32[]{:S(2)}, u32[]{:S(2)}) async-start(bf16[8,34,1024]{2,1,0:T(8,128)(2,1)} %broadcast_multiply_fusion), calls=%async_computation | async-start | bytes 1310720 | tf_op jit(solution)/shard_map/all_to_all | solution.py:60
  60.3 10.1 %all-to-all-start.3 = ((f32[8,1,34]{2,1,0:T(1,128)}), f32[8,1,34]{2,1,0:T(1,128)S(1)}, u32[]{:S(2)}, u32[]{:S(2)}) async-start(f32[8,1,34]{2,1,0:T(1,128)} %all_to_all.31), calls=%async_computation.3 | async-start | bytes 8192 | tf_op jit(solution)/shard_map/all_to_all | solution.py:75
  70.4 9.7 %all-to-all-start.2 = ((f32[8,1,34]{2,1,0:T(1,128)}), f32[8,1,34]{2,1,0:T(1,128)S(1)}, u32[]{:S(2)}, u32[]{:S(2)}) async-start(f32[8,1,34]{2,1,0:T(1,128)} %all_to_all.28), calls=%async_computation.2 | async-start | bytes 8192 | tf_op jit(solution)/shard_map/all_to_all | solution.py:74
where the time goes:
time: 82.7 us; the launch traced here: 82.4 us
  local copies, waits for them, and re-layouts  31.6 us (38%)
  waiting for transfers between devices  22 us (27%)
  starting transfers between devices  17.8 us (22%)
  blocking collectives  7.17 us (9%)
  other arithmetic  2.66 us (3%)
  matrix products  0.84 us (1%)
    scatter x1, local copies, waits for them, and re-layouts, per_device(): jnp.zeros((owners, capacity), jnp.bfloat16).at[targets, slot_index]  9.49 us
    scatter x1, local copies, waits for them, and re-layouts, per_device(): jnp.zeros((owners, capacity), jnp.int32).at[targets, slot_index]  9.28 us
    all_to_all x1, waiting for transfers between devices, per_device(): lax.all_to_all(visitor_rows, 'clus', split_axis=0, concat_axis=0, tiled=T...  8.9 us
    all_to_all x1, starting transfers between devices, per_device(): lax.all_to_all(visitor_inverse, 'clus', split_axis=0, concat_axis=0, tile...  7.28 us
    all_gather x1, blocking collectives, per_device(): cluster_keys = lax.all_gather(normalized, 'rep', axis=0, tiled=True)  7.17 us
    all_to_all x1, waiting for transfers between devices, per_device(): lax.all_to_all(exp_mass, 'clus', split_axis=0, concat_axis=0, tiled=True)  5.39 us
    all_to_all x1, waiting for transfers between devices, per_device(): lax.all_to_all(top_score, 'clus', split_axis=0, concat_axis=0, tiled=True)  4.72 us
    all_to_all x1, starting transfers between devices, per_device(): lax.all_to_all(exp_mass, 'clus', split_axis=0, concat_axis=0, tiled=True)  3.64 us
  transfers between devices with their start and end apart: 4, of which 4 were waited for; matrix products, arithmetic and copies ran while one was open for 7% of the time, Pallas kernels for 0%

commit v1 on v0

--- a/solution.py
+++ b/solution.py
@@ -1,6 +1,10 @@
+import functools
+
 import jax
 import jax.numpy as jnp
 from jax import lax
+from jax.experimental import pallas as pl
+from jax.experimental.pallas import tpu as pltpu
 from jax.sharding import PartitionSpec as P
 
 EPS = 1e-06
@@ -82,9 +86,257 @@
     return (highest + jnp.log(sum_total)) / inv_temp.astype(jnp.float32)
 
 
+NEG = float("-inf")
+RING = (0, 3, 5, 4, 1, 6, 7, 2)
+
+
+def lookup(table, index):
+    value = jnp.int32(table[0])
+    for place in range(1, len(table)):
+        value = jnp.where(index == place, jnp.int32(table[place]), value)
+    return value
+
+
+def dot_nt(left, right):
+    return lax.dot_general(
+        left, right, (((1,), (1,)), ((), ())), preferred_element_type=jnp.float32
+    )
+
+
+def column_stats(scores):
+    top = jnp.max(scores, axis=0, keepdims=True)
+    return top, jnp.sum(jnp.exp(scores - top), axis=0, keepdims=True)
+
+
+def meet_kernel(
+    owners, replicas,
+    emb_ref, inv_ref, routes_ref, out_ref,
+    keys, key_inv, guests, guest_inv, reply, replied, part, parts,
+    key_send, key_recv, kinv_send, kinv_recv, guest_send, guest_recv,
+    ginv_send, ginv_recv, reply_send, reply_recv, part_send, part_recv,
+):
+    rows = emb_ref.shape[0]
+    half = owners // 2
+    cluster = lax.axis_index("clus")
+    rep = lax.axis_index("rep")
+    ring = RING
+    place_of = tuple(ring.index(c) for c in range(owners))
+    place = lookup(place_of, cluster)
+    at = [lookup(ring, lax.rem(place + step, owners)) for step in range(owners)]
+    gives = place >= half
+    peers = [lax.rem(rep + step, replicas) for step in range(replicas)]
+
+    barrier = pltpu.get_barrier_semaphore()
+    for step in range(1, owners):
+        pl.semaphore_signal(barrier, inc=1, device_id=(at[step], rep), device_id_type=pl.DeviceIdType.MESH)
+    for step in range(1, replicas):
+        pl.semaphore_signal(barrier, inc=1, device_id=(cluster, peers[step]), device_id_type=pl.DeviceIdType.MESH)
+
+    widened = emb_ref[...].astype(jnp.float32)
+    scale = lax.rsqrt(jnp.sum(widened * widened, axis=1, keepdims=True) + EPS)
+    unit = (widened * scale).astype(jnp.bfloat16)
+    keys[rep] = unit
+    spread = (
+        lax.broadcasted_iota(jnp.int32, (rows, 2 * rows), 0)
+        == lax.rem(lax.broadcasted_iota(jnp.int32, (rows, 2 * rows), 1), rows)
+    ).astype(jnp.bfloat16)
+    inv_row = jnp.dot(
+        jnp.broadcast_to(inv_ref[...], (16, rows)), spread, preferred_element_type=jnp.float32
+    )[0:8]
+    key_inv[rep] = inv_row
+    inverse = inv_row[0:1, 0:rows]
+    reply[...] = jnp.zeros_like(reply)
+    part[...] = jnp.zeros_like(part)
+
+    def remote(source, target, send, recv, device):
+        return pltpu.make_async_remote_copy(
+            src_ref=source, dst_ref=target, send_sem=send, recv_sem=recv,
+            device_id=device, device_id_type=pl.DeviceIdType.MESH,
+        )
+
+    key_copies, kinv_copies, part_copies = [], [], []
+    for step in range(1, replicas):
+        device = (cluster, peers[step])
+        key_copies.append(remote(keys.at[rep], keys.at[rep], key_send.at[step - 1], key_recv.at[step - 1], device))
+        kinv_copies.append(remote(key_inv.at[rep], key_inv.at[rep], kinv_send.at[step - 1], kinv_recv.at[step - 1], device))
+        part_copies.append(remote(part, parts.at[rep], part_send.at[step - 1], part_recv.at[step - 1], device))
+    guest_copies, ginv_copies, reply_copies = [], [], []
+    for step in range(1, half + 1):
+        slot = step - 1
+        device = (at[step], rep)
+        guest_copies.append(remote(keys.at[rep], guests.at[slot], guest_send.at[slot], guest_recv.at[slot], device))
+        ginv_copies.append(remote(key_inv.at[rep], guest_inv.at[slot], ginv_send.at[slot], ginv_recv.at[slot], device))
+        back = (at[owners - step], rep)
+        reply_copies.append(remote(reply.at[slot], replied.at[slot], reply_send.at[slot], reply_recv.at[slot], back))
+
+    pl.semaphore_wait(barrier, owners - 1 + replicas - 1)
+    for copy in kinv_copies:
+        copy.start()
+    for slot in range(half - 1):
+        ginv_copies[slot].start()
+    for slot in range(max(half - 1, replicas - 1)):
+        if slot < half - 1:
+            guest_copies[slot].start()
+        if slot < replicas - 1:
+            key_copies[slot].start()
+
+    @pl.when(gives)
+    def _():
+        ginv_copies[half - 1].start()
+        guest_copies[half - 1].start()
+
+    diagonal = (
+        lax.broadcasted_iota(jnp.int32, (rows, rows), 0)
+        == lax.broadcasted_iota(jnp.int32, (rows, rows), 1)
+    )
+    routes = routes_ref[...]
+    turned = [
+        jnp.sum(jnp.where(diagonal, routes[:, k : k + 1], 0), axis=0, keepdims=True)
+        for k in range(routes.shape[1])
+    ]
+    hits = [None]
+    for step in range(1, owners):
+        wanted = lax.rem(at[step] - cluster - 1 + owners, owners)
+        hit = turned[0] == wanted
+        for other in turned[1:]:
+            hit = hit | (other == wanted)
+        hits.append(hit)
+
+    for copy in kinv_copies + key_copies:
+        copy.wait_recv()
+    cluster_rows = keys[...].reshape(replicas * rows, keys.shape[2])
+    lane = lax.broadcasted_iota(jnp.int32, (1, 2 * rows), 1)
+    cluster_inv = jnp.concatenate(
+        [
+            jnp.where(lane < rows, key_inv[2 * pair][0:1], key_inv[2 * pair + 1][0:1])
+            for pair in range(replicas // 2)
+        ],
+        axis=1,
+    )
+    own = dot_nt(cluster_rows, keys[rep]) * inverse
+    own = jnp.where(
+        lax.broadcasted_iota(jnp.int32, own.shape, 0)
+        == rep * rows + lax.broadcasted_iota(jnp.int32, own.shape, 1),
+        NEG,
+        own,
+    )
+    own_top, own_mass = column_stats(own)
+
+    def meet(slot):
+        ginv_copies[slot].wait_recv()
+        guest_copies[slot].wait_recv()
+        guest = guests[slot]
+        top, mass = column_stats(dot_nt(cluster_rows, guest) * guest_inv[slot][0:1, 0:rows])
+        reply[slot, 0:1, 0:rows] = top
+        reply[slot, 1:2, 0:rows] = mass
+        reply_copies[slot].start()
+        top, mass = column_stats(dot_nt(guest, cluster_rows) * cluster_inv)
+        part[slot : slot + 1, :] = top
+        part[half + slot : half + slot + 1, :] = mass
+
+    for slot in range(half - 1):
+        meet(slot)
+
+    @pl.when(jnp.logical_not(gives))
+    def _():
+        meet(half - 1)
+
+    for copy in part_copies:
+        copy.start()
+    parts[rep] = part[...]
+
+    for slot in range(half - 1):
+        reply_copies[slot].wait_recv()
+
+    @pl.when(gives)
+    def _():
+        reply_copies[half - 1].wait_recv()
+
+    for copy in part_copies:
+        copy.wait_recv()
+
+    pieces = []
+    for other in range(replicas):
+        whole = parts[other]
+        piece = whole[:, 0 : 2 * rows]
+        for pair in range(1, replicas // 2):
+            piece = jnp.where(rep // 2 == pair, whole[:, 2 * rows * pair : 2 * rows * (pair + 1)], piece)
+        piece = jnp.where(rep % 2 == 1, pltpu.roll(piece, rows, 1), piece)
+        pieces.append(piece[:, 0:rows])
+    part_top = functools.reduce(jnp.maximum, [piece[0:half] for piece in pieces])
+    part_mass = sum(piece[half : 2 * half] * jnp.exp(piece[0:half] - part_top) for piece in pieces)
+
+    found = []
+    for step in range(1, half):
+        found.append((hits[step], replied[step - 1, 0:1, 0:rows], replied[step - 1, 1:2, 0:rows]))
+        found.append((hits[owners - step], part_top[step - 1 : step], part_mass[step - 1 : step]))
+    found.append((
+        hits[half],
+        jnp.where(gives, replied[half - 1, 0:1, 0:rows], part_top[half - 1 : half]),
+        jnp.where(gives, replied[half - 1, 1:2, 0:rows], part_mass[half - 1 : half]),
+    ))
+    highest = own_top
+    for hit, top, _ in found:
+        highest = jnp.maximum(highest, jnp.where(hit, top, NEG))
+    total = own_mass * jnp.exp(own_top - highest)
+    for hit, top, mass in found:
+        total += jnp.where(hit, mass * jnp.exp(top - highest), 0.0)
+    out_ref[...] = (highest + jnp.log(total)) / inverse
+
+    for copy in key_copies + kinv_copies + part_copies:
+        copy.wait_send()
+    for slot in range(half - 1):
+        ginv_copies[slot].wait_send()
+        guest_copies[slot].wait_send()
+        reply_copies[slot].wait_send()
+
+    @pl.when(gives)
+    def _():
+        ginv_copies[half - 1].wait_send()
+        guest_copies[half - 1].wait_send()
+
+    @pl.when(jnp.logical_not(gives))
+    def _():
+        reply_copies[half - 1].wait_send()
+
+
+def meet_per_device(owners, replicas, embeddings, inv_temp, routes):
+    rows, width = embeddings.shape
+    half = owners // 2
+    vmem = pl.BlockSpec(memory_space=pltpu.VMEM)
+    dma = pltpu.SemaphoreType.DMA
+    result = pl.pallas_call(
+        functools.partial(meet_kernel, owners, replicas),
+        out_shape=jax.ShapeDtypeStruct((1, rows), jnp.float32),
+        in_specs=[vmem] * 3,
+        out_specs=vmem,
+        scratch_shapes=[
+            pltpu.VMEM((replicas, rows, width), jnp.bfloat16),
+            pltpu.VMEM((replicas, 8, 2 * rows), jnp.float32),
+            pltpu.VMEM((half, rows, width), jnp.bfloat16),
+            pltpu.VMEM((half, 8, 2 * rows), jnp.float32),
+            pltpu.VMEM((half, 8, 2 * rows), jnp.float32),
+            pltpu.VMEM((half, 8, 2 * rows), jnp.float32),
+            pltpu.VMEM((2 * half, replicas * rows), jnp.float32),
+            pltpu.VMEM((replicas, 2 * half, replicas * rows), jnp.float32),
+        ]
+        + [dma((replicas - 1,))] * 4
+        + [dma((half,))] * 6
+        + [dma((replicas - 1,))] * 2,
+        compiler_params=pltpu.CompilerParams(
+            collective_id=0, has_side_effects=True, vmem_limit_bytes=32 * 1024 * 1024
+        ),
+    )(embeddings, inv_temp.reshape(1, rows), routes)
+    return result.reshape(rows)
+
+
 def solution(mesh):
     in_specs = (P(("clus", "rep"), None), P(("clus", "rep")), P(("clus", "rep"), None))
     out_specs = P(("clus", "rep"))
+    owners, replicas = mesh.shape["clus"], mesh.shape["rep"]
+    body = per_device
+    if owners == len(RING) and replicas == 4:
+        body = functools.partial(meet_per_device, owners, replicas)
     return jax.shard_map(
-        per_device, mesh=mesh, in_specs=in_specs, out_specs=out_specs, check_vma=False
-    )
+        body, mesh=mesh, in_specs=in_specs, out_specs=out_specs, check_vma=False
+    )

time: 82.7 us -> 25.4 us (0.31)
  local copies, waits for them, and re-layouts: 31.6 us -> 2.2 us
  Pallas kernels: 0 us -> 23.1 us
  waiting for transfers between devices: 22 us -> 0 us
  starting transfers between devices: 17.8 us -> 0 us
  blocking collectives: 7.17 us -> 0 us
  other arithmetic: 2.66 us -> 0 us
  matrix products: 0.84 us -> 0 us
    pallas_call x0 -> x1, Pallas kernels: none -> 23.1 us  [meet_per_device(): pl.pallas_call(functools.partial(meet_kernel, owners, replicas), out_shap...]
    all_to_all x4 -> x0, waiting for transfers between devices: 22 us -> none  [the longest x1 8.9 us: per_device(): lax.all_to_all(visitor_rows, 'clus', split_axis=0, concat_axis=0, tiled=T...]
    scatter x2 -> x0, local copies, waits for them, and re-layouts: 18.8 us -> none  [the longest x1 9.49 us: per_device(): jnp.zeros((owners, capacity), jnp.bfloat16).at[targets, slot_index]]
    all_to_all x4 -> x0, starting transfers between devices: 17.8 us -> none  [the longest x1 7.28 us: per_device(): lax.all_to_all(visitor_inverse, 'clus', split_axis=0, concat_axis=0, tile...]
    gather x11 -> x0, local copies, waits for them, and re-layouts: 9.22 us -> none  [the longest x2 2.45 us: per_device(): visitor_inverse = inv_temp[source_table] * filled]
    all_gather x1 -> x0, blocking collectives: 7.17 us -> none  [per_device(): cluster_keys = lax.all_gather(normalized, 'rep', axis=0, tiled=True)]
    all_to_all x3 -> x0, local copies, waits for them, and re-layouts: 1.95 us -> none  [the longest x1 0.69 us: per_device(): lax.all_to_all(top_score, 'clus', split_axis=0, concat_axis=0, tiled=True)]
    unnamed x7 -> x6, local copies, waits for them, and re-layouts: 0.79 us -> 2.2 us
  transfers between devices with their start and end apart: 4 -> 0, of which waited for: 4 -> 0; matrix products, arithmetic and copies ran while one was open for 7% -> 0% of each run, Pallas kernels for 0% -> 0%
where the time goes in v1:
time: 25.4 us; the launch traced here: 25.3 us
  Pallas kernels  23.1 us (91%)
  local copies, waits for them, and re-layouts  2.2 us (9%)
    pallas_call x1, Pallas kernels, meet_per_device(): pl.pallas_call(functools.partial(meet_kernel, owners, replicas), out_shap...  23.1 us
    unnamed x6, local copies, waits for them, and re-layouts  2.2 us

profile of v1, /device:TPU:0, one launch (start us, length us, event | category | flops | bytes accessed | tf_op | source)
XLA Modules:
  0.0 25.3 jit_solution(9607225382570796734)
XLA Ops:
  0.0 0.0 copy-start.1
  0.0 0.8 %copy.4.routes_ref = s32[64,3]{1,0:T(8,128)S(1)} copy(s32[64,3]{0,1:T(4,128)} %param.5) | data formatting | bytes 1536 | tf_op args[2]
  0.8 0.0 copy-done.1
  0.8 0.0 copy-start
  0.8 0.9 %copy-done = bf16[64,1024]{1,0:T(8,128)(2,1)S(1)} copy-done((bf16[64,1024]{1,0:T(8,128)(2,1)S(1)}, bf16[64,1024]{1,0:T(8,128)(2,1)}, u32[]{:S(2)}) %copy-start) | copy-done | bytes 131096
  1.7 23.1 %shard_map.37 = f32[1,64]{1,0:T(1,128)S(1)} custom-call(bf16[64,1024]{1,0:T(8,128)(2,1)S(1)} %copy-done, bf16[1,64]{1,0:T(2,128)(2,1)S(1)} %bitcast.2, s32[64,3]{1,0:T(8,128)S(1)} %copy.4.routes_ref), custom_call_target="tpu_custom_call" | custom-call | tf_op jit(solution)/shard_map/pallas_call | solution.py:308
  24.8 0.5 %copy.6 = f32[64]{0:T(128)} copy(f32[64]{0:T(128)S(1)} %bitcast.3) | data formatting | bytes 512
Async XLA Ops:
  0.0 0.8 %copy-start.1 = (bf16[64]{0:T(256)(128)(2,1)S(1)}, bf16[64]{0:T(256)(128)(2,1)}, u32[]{:S(2)}) copy-start(bf16[64]{0:T(256)(128)(2,1)} %param.4) | copy-start | bytes 388
  0.8 0.9 %copy-start = (bf16[64,1024]{1,0:T(8,128)(2,1)S(1)}, bf16[64,1024]{1,0:T(8,128)(2,1)}, u32[]{:S(2)}) copy-start(bf16[64,1024]{1,0:T(8,128)(2,1)} %emb_ref.1) | copy-start | bytes 393220

commit v2 on v1

--- a/solution.py
+++ b/solution.py
@@ -87,7 +87,9 @@
 
 
 NEG = float("-inf")
-RING = (0, 3, 5, 4, 1, 6, 7, 2)
+RING = (0, 4, 1, 5, 2, 6, 3, 7)
+GIVERS = (1, 0, 1, 0, 0, 1, 0, 1)
+PIECES = 4
 
 
 def lookup(table, index):
@@ -110,12 +112,20 @@
 
 def meet_kernel(
     owners, replicas,
-    emb_ref, inv_ref, routes_ref, out_ref,
+    emb_hbm, inv_hbm, routes_hbm, out_ref, emb_ref, inv_ref, routes_ref,
     keys, key_inv, guests, guest_inv, reply, replied, part, parts,
     key_send, key_recv, kinv_send, kinv_recv, guest_send, guest_recv,
-    ginv_send, ginv_recv, reply_send, reply_recv, part_send, part_recv,
+    ginv_send, ginv_recv, reply_send, reply_recv, part_send, part_recv, fetch_sem,
 ):
     rows = emb_ref.shape[0]
+    fetches = [
+        pltpu.make_async_copy(source, target, fetch_sem.at[k])
+        for k, (source, target) in enumerate(
+            ((emb_hbm, emb_ref), (inv_hbm, inv_ref), (routes_hbm, routes_ref))
+        )
+    ]
+    for fetch in fetches:
+        fetch.start()
     half = owners // 2
     cluster = lax.axis_index("clus")
     rep = lax.axis_index("rep")
@@ -123,7 +133,8 @@
     place_of = tuple(ring.index(c) for c in range(owners))
     place = lookup(place_of, cluster)
     at = [lookup(ring, lax.rem(place + step, owners)) for step in range(owners)]
-    gives = place >= half
+    gives = lookup(GIVERS, place) == 1
+    hands = lookup(GIVERS, lax.rem(place + owners - 1, owners)) == 1
     peers = [lax.rem(rep + step, replicas) for step in range(replicas)]
 
     barrier = pltpu.get_barrier_semaphore()
@@ -132,6 +143,8 @@
     for step in range(1, replicas):
         pl.semaphore_signal(barrier, inc=1, device_id=(cluster, peers[step]), device_id_type=pl.DeviceIdType.MESH)
 
+    for fetch in fetches:
+        fetch.wait()
     widened = emb_ref[...].astype(jnp.float32)
     scale = lax.rsqrt(jnp.sum(widened * widened, axis=1, keepdims=True) + EPS)
     unit = (widened * scale).astype(jnp.bfloat16)
@@ -160,40 +173,43 @@
         key_copies.append(remote(keys.at[rep], keys.at[rep], key_send.at[step - 1], key_recv.at[step - 1], device))
         kinv_copies.append(remote(key_inv.at[rep], key_inv.at[rep], kinv_send.at[step - 1], kinv_recv.at[step - 1], device))
         part_copies.append(remote(part, parts.at[rep], part_send.at[step - 1], part_recv.at[step - 1], device))
+    size = rows // PIECES
     guest_copies, ginv_copies, reply_copies = [], [], []
     for step in range(1, half + 1):
         slot = step - 1
         device = (at[step], rep)
-        guest_copies.append(remote(keys.at[rep], guests.at[slot], guest_send.at[slot], guest_recv.at[slot], device))
+        relayed = step > 2
+        target = (at[step - 1], rep) if relayed else device
+        origin = guests.at[0] if relayed else keys.at[rep]
+        guest_copies.append([
+            remote(
+                origin.at[pl.ds(piece * size, size)], guests.at[slot, pl.ds(piece * size, size)],
+                guest_send.at[slot, piece], guest_recv.at[slot, piece], target,
+            )
+            for piece in range(PIECES)
+        ])
         ginv_copies.append(remote(key_inv.at[rep], guest_inv.at[slot], ginv_send.at[slot], ginv_recv.at[slot], device))
         back = (at[owners - step], rep)
         reply_copies.append(remote(reply.at[slot], replied.at[slot], reply_send.at[slot], reply_recv.at[slot], back))
 
     pl.semaphore_wait(barrier, owners - 1 + replicas - 1)
+    for copy in guest_copies[0]:
+        copy.start()
     for copy in kinv_copies:
+        copy.start()
+    for copy in key_copies:
+        copy.start()
+    for copy in guest_copies[1]:
         copy.start()
     for slot in range(half - 1):
         ginv_copies[slot].start()
-    for slot in range(max(half - 1, replicas - 1)):
-        if slot < half - 1:
-            guest_copies[slot].start()
-        if slot < replicas - 1:
-            key_copies[slot].start()
 
     @pl.when(gives)
     def _():
         ginv_copies[half - 1].start()
-        guest_copies[half - 1].start()
-
-    diagonal = (
-        lax.broadcasted_iota(jnp.int32, (rows, rows), 0)
-        == lax.broadcasted_iota(jnp.int32, (rows, rows), 1)
-    )
+
     routes = routes_ref[...]
-    turned = [
-        jnp.sum(jnp.where(diagonal, routes[:, k : k + 1], 0), axis=0, keepdims=True)
-        for k in range(routes.shape[1])
-    ]
+    turned = [routes[k : k + 1] for k in range(routes.shape[0])]
     hits = [None]
     for step in range(1, owners):
         wanted = lax.rem(at[step] - cluster - 1 + owners, owners)
@@ -201,6 +217,14 @@
         for other in turned[1:]:
             hit = hit | (other == wanted)
         hits.append(hit)
+
+    for piece in range(PIECES):
+        guest_copies[0][piece].wait_recv()
+        guest_copies[2][piece].start()
+
+        @pl.when(hands)
+        def _():
+            guest_copies[3][piece].start()
 
     for copy in kinv_copies + key_copies:
         copy.wait_recv()
@@ -224,7 +248,9 @@
 
     def meet(slot):
         ginv_copies[slot].wait_recv()
-        guest_copies[slot].wait_recv()
+        if slot > 0:
+            for copy in guest_copies[slot]:
+                copy.wait_recv()
         guest = guests[slot]
         top, mass = column_stats(dot_nt(cluster_rows, guest) * guest_inv[slot][0:1, 0:rows])
         reply[slot, 0:1, 0:rows] = top
@@ -287,13 +313,18 @@
         copy.wait_send()
     for slot in range(half - 1):
         ginv_copies[slot].wait_send()
-        guest_copies[slot].wait_send()
         reply_copies[slot].wait_send()
+        for copy in guest_copies[slot]:
+            copy.wait_send()
+
+    @pl.when(hands)
+    def _():
+        for copy in guest_copies[half - 1]:
+            copy.wait_send()
 
     @pl.when(gives)
     def _():
         ginv_copies[half - 1].wait_send()
-        guest_copies[half - 1].wait_send()
 
     @pl.when(jnp.logical_not(gives))
     def _():
@@ -308,9 +339,12 @@
     result = pl.pallas_call(
         functools.partial(meet_kernel, owners, replicas),
         out_shape=jax.ShapeDtypeStruct((1, rows), jnp.float32),
-        in_specs=[vmem] * 3,
+        in_specs=[pl.BlockSpec(memory_space=pl.ANY)] * 3,
         out_specs=vmem,
         scratch_shapes=[
+            pltpu.VMEM((rows, width), jnp.bfloat16),
+            pltpu.VMEM((1, rows), inv_temp.dtype),
+            pltpu.VMEM((routes.shape[1], rows), routes.dtype),
             pltpu.VMEM((replicas, rows, width), jnp.bfloat16),
             pltpu.VMEM((replicas, 8, 2 * rows), jnp.float32),
             pltpu.VMEM((half, rows, width), jnp.bfloat16),
@@ -321,12 +355,14 @@
             pltpu.VMEM((replicas, 2 * half, replicas * rows), jnp.float32),
         ]
         + [dma((replicas - 1,))] * 4
-        + [dma((half,))] * 6
-        + [dma((replicas - 1,))] * 2,
+        + [dma((half, PIECES))] * 2
+        + [dma((half,))] * 4
+        + [dma((replicas - 1,))] * 2
+        + [dma((3,))],
         compiler_params=pltpu.CompilerParams(
-            collective_id=0, has_side_effects=True, vmem_limit_bytes=32 * 1024 * 1024
+            collective_id=0, has_side_effects=True, vmem_limit_bytes=60 * 1024 * 1024
         ),
-    )(embeddings, inv_temp.reshape(1, rows), routes)
+    )(embeddings, inv_temp.reshape(1, rows), routes.T)
     return result.reshape(rows)
 
 

time: 25.4 us -> 23.6 us (0.929)
  local copies, waits for them, and re-layouts: 2.2 us -> 1.1 us
  Pallas kernels: 23.1 us -> 22.3 us
    unnamed x6 -> x3, local copies, waits for them, and re-layouts: 2.2 us -> 1.1 us
    pallas_call x1, Pallas kernels: 23.1 us -> 22.3 us  [meet_per_device(): pl.pallas_call(functools.partial(meet_kernel, owners, replicas), out_shap...]
where the time goes in v2:
time: 23.6 us; the launch traced here: 23.5 us
  Pallas kernels  22.3 us (94%)
  local copies, waits for them, and re-layouts  1.1 us (5%)
    pallas_call x1, Pallas kernels, meet_per_device(): pl.pallas_call(functools.partial(meet_kernel, owners, replicas), out_shap...  22.3 us
    unnamed x3, local copies, waits for them, and re-layouts  1.1 us

profile of v2, /device:TPU:0, one launch (start us, length us, event | category | flops | bytes accessed | tf_op | source)
XLA Modules:
  0.0 23.5 jit_solution(16952136897219597769)
XLA Ops:
  0.0 22.3 %shard_map.37 = f32[1,64]{1,0:T(1,128)} custom-call(bf16[64,1024]{1,0:T(8,128)(2,1)} %emb_hbm.1, bf16[1,64]{1,0:T(2,128)(2,1)} %bitcast.4, s32[3,64]{1,0:T(4,128)} %bitcast.3), custom_call_target="tpu_custom_call" | custom-call | tf_op jit(solution)/shard_map/pallas_call | solution.py:339
  22.4 0.0 copy-start
  22.4 0.6 %copy-done = f32[1,64]{1,0:T(1,128)S(1)} copy-done((f32[1,64]{1,0:T(1,128)S(1)}, f32[1,64]{1,0:T(1,128)}, u32[]{:S(2)}) %copy-start) | copy-done | bytes 280
  23.0 0.5 %copy.5 = f32[64]{0:T(128)} copy(f32[64]{0:T(128)S(1)} %bitcast.5) | data formatting | bytes 512
Async XLA Ops:
  22.4 0.6 %copy-start = (f32[1,64]{1,0:T(1,128)S(1)}, f32[1,64]{1,0:T(1,128)}, u32[]{:S(2)}) copy-start(f32[1,64]{1,0:T(1,128)} %shard_map.37) | copy-start | bytes 772
